TPU v7x, 32 devices: a whole 2x2x4 slice. The times are simulated.
32 devices in a mesh: blk: 8 (over z, x), col: 4 (over y, core).
Axes of the slice: x: 2, y: 2, z: 4, core: 2. Of those that a mesh axis runs over, the one named last changes fastest.
Arguments:
- density: float32 [2048, 1024], P('blk'), may hold values from -0.1875 to 0.1875
- occupied_p: int32 [16, 8], P('blk'), may hold values 0 or 1
- hamil_dens: float32 [1024, 2048], P('blk', 'col'), may hold values from -6 to 6
- occupied_hp: int32 [8, 16], P('blk', 'col'), may hold values 0 or 1
- window_sizes: int32 [8], replicated, may hold values from 64 to 128
- row_window_sizes: int32 [16], replicated, may hold values from 64 to 128
- slab_index: int32 [16], P('col'), may hold values from 0 to 781
- group_sizes: int32 [782], replicated, may hold values from 64 to 128
Outputs:
- product: float32 [2048, 2048], P('blk', 'col')
- norm_sq: float32 [], replicated
All inputs are finite; a program needn't handle non-finite values. No bound on the sum of `occupied_p` or of `occupied_hp` on one device may be relied on, other than what follows from the above.
Results may differ from a plain program's by a relative error of at most 0.000068.
Values sent between devices are 32-bit elements; how exact they have to be, the bound alone decides.
A program may use at most 64 MiB of HBM per device.

v0:
```python
import functools

import jax
import jax.numpy as jnp
from jax import lax
from jax.experimental import pallas as pl
from jax.experimental.pallas import tpu as pltpu
from jax.sharding import PartitionSpec as P

MESH = pl.DeviceIdType.MESH
PAIR = 2
CHUNKS = 4
EXTRA = 1


def kernel(
    length,
    cols,
    density,
    hamil_in,
    occ_p_in,
    occ_hp_in,
    window_in,
    row_window_in,
    slab_in,
    groups_in,
    product_out,
    norm,
    product,
    hamil,
    occ_p,
    occ_hp,
    window,
    row_window,
    slab,
    groups,
    gathered,
    p_in,
    p_high,
    p_low,
    parts,
    col_parts,
    send_sem,
    recv_sem,
    load_sem,
    part_send,
    part_recv,
    col_send,
    col_recv,
):
    count = length * PAIR
    block, width = hamil.shape
    row_blocks = product.shape[0] // block
    panels = width // block
    piece = block // CHUNKS
    me = lax.axis_index("blk")
    my_col = lax.axis_index("col")
    z = me // PAIR
    x = me % PAIR
    partner = me + 1 - 2 * x
    has_up = z < length - 1
    has_down = z > 0

    loads = [
        pltpu.make_async_copy(source, target, load_sem.at[at])
        for at, (source, target) in enumerate(
            (
                (hamil_in, hamil),
                (occ_hp_in, occ_hp),
                (window_in, window),
                (slab_in, slab),
                (groups_in, groups),
                (row_window_in, row_window),
                (occ_p_in, occ_p),
                (density, p_in),
            )
        )
    ]
    barrier = pltpu.get_barrier_semaphore()

    @pl.loop(1, count)
    def greet_blk(step):
        pl.semaphore_signal(
            barrier, inc=1, device_id={"blk": (me + step) % count}, device_id_type=MESH
        )

    @pl.loop(1, cols)
    def greet_col(step):
        pl.semaphore_signal(
            barrier, inc=1, device_id={"col": (my_col + step) % cols}, device_id_type=MESH
        )

    for load in loads:
        load.start()

    for load in loads[:5]:
        load.wait()

    row_at = lax.broadcasted_iota(jnp.int32, (block, block), 0)
    col_at = lax.broadcasted_iota(jnp.int32, (block, block), 1)
    rows_live = row_at < window[me]
    for panel in range(panels):
        size = groups[slab[panel]]
        occupied = occ_hp[0, panel].astype(jnp.float32)
        mask = jnp.where(rows_live & (col_at < size), occupied, 0.0)
        here = pl.ds(panel * block, block)
        gathered[me, :, here] = hamil[:, here] * mask

    pl.semaphore_wait(barrier, count - 1 + cols - 1)

    def move(where, k, chunk, device):
        rows = gathered.at[k, pl.ds(chunk * piece, piece), :]
        return pltpu.make_async_remote_copy(
            src_ref=rows,
            dst_ref=rows,
            send_sem=send_sem.at[where, k, chunk],
            recv_sem=recv_sem.at[k, chunk],
            device_id={"blk": device},
            device_id_type=MESH,
        )

    def up(k, chunk):
        return move(0, k, chunk, me + PAIR)

    def down(k, chunk):
        return move(1, k, chunk, me - PAIR)

    def across(k, chunk):
        return move(2, k, chunk, partner)

    for chunk in range(CHUNKS):
        across(me, chunk).start()

        @pl.when(has_up)
        def _():
            up(me, chunk).start()

        @pl.when(has_down)
        def _():
            down(me, chunk).start()

    for load in loads[5:]:
        load.wait()

    @pl.loop(0, length)
    def split(at):
        for b in range(row_blocks):
            live = row_at < row_window[me * row_blocks + b]
            here = pl.ds(b * block, block)
            for other in range(PAIR):
                k = at * PAIR + other
                mask = jnp.where(
                    live & (col_at < window[k]), occ_p[b, k].astype(jnp.float32), 0.0
                )
                value = p_in[here, pl.ds(pl.multiple_of(k * block, block), block)] * mask
                high = value.astype(jnp.bfloat16)
                there = pl.ds(other * block, block)
                p_high[at, here, there] = high
                p_low[at, here, there] = (value - high.astype(jnp.float32)).astype(jnp.bfloat16)

    def term(at, first):
        right = gathered[pl.ds(at * PAIR, PAIR)].reshape(PAIR * block, width)
        high = right.astype(jnp.bfloat16)
        low = (right - high.astype(jnp.float32)).astype(jnp.bfloat16)

        def times(a, b):
            return jnp.dot(a, b, preferred_element_type=jnp.float32)

        left = p_high[at]
        value = times(left, low) + times(p_low[at], high) + times(left, high)
        product[...] = value if first else product[...] + value

    for chunk in range(EXTRA):
        across(partner, chunk).wait_recv()

        @pl.when(has_up)
        def _():
            up(partner, chunk).start()

        @pl.when(has_down)
        def _():
            down(partner, chunk).start()

    def pass_on(distance):
        for chunk in range(CHUNKS):

            @pl.when(z - distance >= 0)
            def _():
                k = me - distance * PAIR
                across(k, chunk).wait_recv()

                @pl.when(has_up)
                def _():
                    up(k, chunk).start()

                if chunk < EXTRA:

                    @pl.when(distance > 1)
                    def _():
                        across(k, chunk).start()

                else:
                    across(k, chunk).start()

            @pl.when(z + distance < length)
            def _():
                k = me + distance * PAIR
                across(k, chunk).wait_recv()

                @pl.when(has_down)
                def _():
                    down(k, chunk).start()

                if chunk < EXTRA:

                    @pl.when(distance > 1)
                    def _():
                        across(k, chunk).start()

                else:
                    across(k, chunk).start()

    def add_terms(distance):
        for sign in (-1, 1):
            at = z + sign * distance

            @pl.when((at >= 0) & (at < length))
            def _():
                for chunk in range(CHUNKS):
                    across(partner + sign * distance * PAIR, chunk).wait_recv()
                term(at, False)

    if length > 1:
        pass_on(1)

    for chunk in range(EXTRA, CHUNKS):
        across(partner, chunk).wait_recv()
    term(z, True)

    @pl.loop(2, length)
    def steps(distance):
        pass_on(distance)

    @pl.loop(1, length)
    def products(distance):
        add_terms(distance)

    store = pltpu.make_async_copy(product, product_out, load_sem.at[0])
    store.start()

    squares = product[...] * product[...]
    squares = jnp.sum(squares.reshape(squares.shape[0] // 8, 8, width), axis=0)
    total = squares[:, :128]
    for panel in range(1, width // 128):
        total = total + squares[:, panel * 128 : (panel + 1) * 128]
    parts[me] = total

    def part_to(device):
        return pltpu.make_async_remote_copy(
            src_ref=parts.at[me],
            dst_ref=parts.at[me],
            send_sem=part_send.at[device],
            recv_sem=part_recv.at[me],
            device_id={"blk": device},
            device_id_type=MESH,
        )

    def part_from(device):
        return pltpu.make_async_remote_copy(
            src_ref=parts.at[device],
            dst_ref=parts.at[device],
            send_sem=part_send.at[device],
            recv_sem=part_recv.at[device],
            device_id={"blk": device},
            device_id_type=MESH,
        )

    @pl.loop(1, count)
    def send_parts(step):
        part_to((me + step) % count).start()

    @pl.loop(0, length)
    def sent(at):
        k = at * PAIR + x
        far = (at - z > 1) | (z - at > 1) | (at == z)
        for chunk in range(CHUNKS):

            @pl.when(has_up & (at <= z))
            def _():
                up(k, chunk).wait_send()

            @pl.when(has_down & (at >= z))
            def _():
                down(k, chunk).wait_send()

            if chunk < EXTRA:

                @pl.when(far)
                def _():
                    across(k, chunk).wait_send()

            else:
                across(k, chunk).wait_send()

    for chunk in range(EXTRA):

        @pl.when(has_up)
        def _():
            up(partner, chunk).wait_send()

        @pl.when(has_down)
        def _():
            down(partner, chunk).wait_send()

    @pl.loop(1, count)
    def get_parts(step):
        part_from((me + step) % count).wait_recv()

    col_parts[my_col] = jnp.sum(parts[...], axis=0)

    def col_to(device):
        return pltpu.make_async_remote_copy(
            src_ref=col_parts.at[my_col],
            dst_ref=col_parts.at[my_col],
            send_sem=col_send.at[device],
            recv_sem=col_recv.at[my_col],
            device_id={"col": device},
            device_id_type=MESH,
        )

    def col_from(device):
        return pltpu.make_async_remote_copy(
            src_ref=col_parts.at[device],
            dst_ref=col_parts.at[device],
            send_sem=col_send.at[device],
            recv_sem=col_recv.at[device],
            device_id={"col": device},
            device_id_type=MESH,
        )

    @pl.loop(1, cols)
    def send_cols(step):
        col_to((my_col + step) % cols).start()

    @pl.loop(1, count)
    def sent_parts(step):
        part_to((me + step) % count).wait_send()

    @pl.loop(1, cols)
    def get_cols(step):
        col_from((my_col + step) % cols).wait_recv()

    store.wait()
    norm[0] = jnp.sum(jnp.sum(col_parts[...], axis=0))

    @pl.loop(1, cols)
    def sent_cols(step):
        col_to((my_col + step) % cols).wait_send()


def solution(mesh):
    count = mesh.shape["blk"]
    cols = mesh.shape["col"]
    length = count // PAIR

    def per_device(
        density,
        occupied_p,
        hamil_dens,
        occupied_hp,
        window_sizes,
        row_window_sizes,
        slab_index,
        group_sizes,
    ):
        rows, inner = density.shape
        block, width = hamil_dens.shape
        hbm = pl.BlockSpec(memory_space=pltpu.HBM)
        smem = pl.BlockSpec(memory_space=pltpu.SMEM)
        product, norm = pl.pallas_call(
            functools.partial(kernel, length, cols),
            out_shape=(
                jax.ShapeDtypeStruct((rows, width), jnp.float32),
                jax.ShapeDtypeStruct((1,), jnp.float32),
            ),
            in_specs=[hbm] * 8,
            out_specs=(hbm, smem),
            scratch_shapes=[
                pltpu.VMEM((rows, width), jnp.float32),
                pltpu.VMEM((block, width), jnp.float32),
                pltpu.SMEM(occupied_p.shape, jnp.int32),
                pltpu.SMEM(occupied_hp.shape, jnp.int32),
                pltpu.SMEM(window_sizes.shape, jnp.int32),
                pltpu.SMEM(row_window_sizes.shape, jnp.int32),
                pltpu.SMEM(slab_index.shape, jnp.int32),
                pltpu.SMEM(group_sizes.shape, jnp.int32),
                pltpu.VMEM((count, block, width), jnp.float32),
                pltpu.VMEM((rows, inner), jnp.float32),
                pltpu.VMEM((length, rows, PAIR * block), jnp.bfloat16),
                pltpu.VMEM((length, rows, PAIR * block), jnp.bfloat16),
                pltpu.VMEM((count, 8, 128), jnp.float32),
                pltpu.VMEM((cols, 8, 128), jnp.float32),
                pltpu.SemaphoreType.DMA((3, count, CHUNKS)),
                pltpu.SemaphoreType.DMA((count, CHUNKS)),
                pltpu.SemaphoreType.DMA((8,)),
                pltpu.SemaphoreType.DMA((count,)),
                pltpu.SemaphoreType.DMA((count,)),
                pltpu.SemaphoreType.DMA((cols,)),
                pltpu.SemaphoreType.DMA((cols,)),
            ],
            compiler_params=pltpu.CompilerParams(
                collective_id=0, has_side_effects=True, vmem_limit_bytes=56 << 20
            ),
        )(
            density,
            hamil_dens,
            occupied_p,
            occupied_hp,
            window_sizes,
            row_window_sizes,
            slab_index,
            group_sizes,
        )
        return product, norm.reshape(())

    return jax.shard_map(
        per_device,
        mesh=mesh,
        in_specs=(
            P("blk", None),
            P("blk", None),
            P("blk", "col"),
            P("blk", "col"),
            P(),
            P(),
            P("col"),
            P(),
        ),
        out_specs=(P("blk", "col"), P()),
        check_vma=False,
    )
```

profile of v0, /device:TPU:0, one launch (start us, length us, event | category | flops | bytes accessed | tf_op | source)
XLA Modules:
  0.0 42.4 jit_solution(3578357559068543912)
XLA Ops:
  0.6 38.2 %shard_map.95 = (f32[256,512]{1,0:T(8,128)}, f32[1]{0:T(128)}) custom-call(f32[256,1024]{1,0:T(8,128)} %density.1, f32[128,512]{1,0:T(8,128)} %hamil_in.1, s32[2,8]{1,0:T(2,128)} %occ_p_in.1, s32[1,4]{1,0:T(1,128)} %occ_hp_in.1, s32[8]{0:T(128)} %window_in.1, s32[16]{0:T(128)} %row_window_in.1, s32[4]{0:T(128)} %slab_in.1, s32[782]{0:T(1024)} %groups_in.1), custom_call_target="tpu_custom_call" | custom-call | tf_op jit(solution)/shard_map/pallas_call | solution.py:380
  38.8 1.9 %copy.12 = f32[256,512]{1,0:T(8,128)} copy(f32[256,512]{1,0:T(8,128)} %get-tuple-element.8) | data formatting | bytes 1048576
where the time goes:
time: 42.6 us; the launch traced here: 42.4 us
  Pallas kernels  38.2 us (90%)
  between operations  2.34 us (5%)
  local copies, waits for them, and re-layouts  1.87 us (4%)
    pallas_call x1, Pallas kernels, per_device(): pl.pallas_call(functools.partial(kernel, length, cols), out_shape=(jax.Sh...  38.2 us
    unnamed x1, local copies, waits for them, and re-layouts  1.87 us

commit v1 on v0

v1 whole, which is shorter than its diff:
```python
import functools

import jax
import jax.numpy as jnp
from jax import lax
from jax.experimental import pallas as pl
from jax.experimental.pallas import tpu as pltpu
from jax.sharding import PartitionSpec as P

MESH = pl.DeviceIdType.MESH
PAIR = 2
CHUNKS = 4
EXTRA = 2


def kernel(
    length,
    cols,
    density,
    hamil_in,
    occ_p_in,
    occ_hp_in,
    window_in,
    row_window_in,
    slab_in,
    groups_in,
    product,
    norm,
    hamil,
    occ_p,
    occ_hp,
    window,
    row_window,
    slab,
    groups,
    gathered,
    p_in,
    p_high,
    p_low,
    parts,
    send_sem,
    recv_sem,
    load_sem,
    part_send,
    part_recv,
):
    count = length * PAIR
    total = count * cols
    block, width = hamil.shape
    row_blocks = product.shape[0] // block
    panels = width // block
    piece = block // CHUNKS
    me = lax.axis_index("blk")
    my_col = lax.axis_index("col")
    z = me // PAIR
    x = me % PAIR
    partner = me + 1 - 2 * x
    last = length - 1
    has_up = z < last
    has_down = z > 0

    loads = [
        pltpu.make_async_copy(source, target, load_sem.at[at])
        for at, (source, target) in enumerate(
            (
                (occ_hp_in, occ_hp),
                (window_in, window),
                (slab_in, slab),
                (groups_in, groups),
                (row_window_in, row_window),
                (occ_p_in, occ_p),
                (density, p_in),
            )
        )
    ]
    hamil_loads = [
        pltpu.make_async_copy(
            hamil_in.at[pl.ds(chunk * piece, piece)],
            hamil.at[pl.ds(chunk * piece, piece)],
            load_sem.at[len(loads) + chunk],
        )
        for chunk in range(CHUNKS)
    ]
    barrier = pltpu.get_barrier_semaphore()

    def greet(device):
        pl.semaphore_signal(barrier, inc=1, device_id=device, device_id_type=MESH)

    greet({"blk": partner})

    @pl.when(has_up)
    def _():
        greet({"blk": me + PAIR})

    @pl.when(has_down)
    def _():
        greet({"blk": me - PAIR})

    @pl.loop(1, cols)
    def greet_col(step):
        greet({"col": (my_col + step) % cols})

    for load in loads[:4] + hamil_loads + loads[4:]:
        load.start()

    for load in loads[:4]:
        load.wait()

    def move(where, k, chunk, device):
        rows = gathered.at[k, pl.ds(chunk * piece, piece), :]
        return pltpu.make_async_remote_copy(
            src_ref=rows,
            dst_ref=rows,
            send_sem=send_sem.at[where, k, chunk],
            recv_sem=recv_sem.at[k, chunk],
            device_id={"blk": device},
            device_id_type=MESH,
        )

    def up(k, chunk):
        return move(0, k, chunk, me + PAIR)

    def down(k, chunk):
        return move(1, k, chunk, me - PAIR)

    def across(k, chunk):
        return move(2, k, chunk, partner)

    piece_row = lax.broadcasted_iota(jnp.int32, (piece, block), 0)
    piece_col = lax.broadcasted_iota(jnp.int32, (piece, block), 1)
    order = list(range(EXTRA, CHUNKS)) + list(range(EXTRA))
    for at, chunk in enumerate(order):
        hamil_loads[chunk].wait()
        there = pl.ds(chunk * piece, piece)
        rows_live = piece_row + chunk * piece < window[me]
        for panel in range(panels):
            size = groups[slab[panel]]
            occupied = occ_hp[0, panel].astype(jnp.float32)
            mask = jnp.where(rows_live & (piece_col < size), occupied, 0.0)
            here = pl.ds(panel * block, block)
            gathered[me, there, here] = hamil[there, here] * mask
        if at == 0:
            ends = jnp.int32(z == 0) + jnp.int32(z == last)
            pl.semaphore_wait(barrier, PAIR - 1 + cols - 1 + 2 - ends)

        across(me, chunk).start()

        @pl.when(has_up)
        def _():
            up(me, chunk).start()

        @pl.when(has_down)
        def _():
            down(me, chunk).start()

    for load in loads[4:]:
        load.wait()

    row_at = lax.broadcasted_iota(jnp.int32, (block, block), 0)
    col_at = lax.broadcasted_iota(jnp.int32, (block, block), 1)

    @pl.loop(0, length)
    def split(at):
        for b in range(row_blocks):
            live = row_at < row_window[me * row_blocks + b]
            here = pl.ds(b * block, block)
            for other in range(PAIR):
                k = at * PAIR + other
                mask = jnp.where(
                    live & (col_at < window[k]), occ_p[b, k].astype(jnp.float32), 0.0
                )
                value = p_in[here, pl.ds(pl.multiple_of(k * block, block), block)] * mask
                high = value.astype(jnp.bfloat16)
                there = pl.ds(other * block, block)
                p_high[at, here, there] = high
                p_low[at, here, there] = (value - high.astype(jnp.float32)).astype(jnp.bfloat16)

    def times(a, b):
        return jnp.dot(a, b, preferred_element_type=jnp.float32)

    def term(at, first):
        for chunk in range(CHUNKS):
            if chunk < EXTRA:

                @pl.when((at > 0) & (at < last))
                def _():
                    across(at * PAIR + 1 - x, chunk).wait_recv()

            else:
                across(at * PAIR + 1 - x, chunk).wait_recv()
        right = gathered[pl.ds(at * PAIR, PAIR)].reshape(PAIR * block, width)
        high = right.astype(jnp.bfloat16)
        low = (right - high.astype(jnp.float32)).astype(jnp.bfloat16)
        left = p_high[at]
        value = times(left, low) + times(p_low[at], high) + times(left, high)
        product[...] = value if first else product[...] + value

    def pass_line(distance):
        for chunk in order:

            @pl.when(z - distance >= 0)
            def _():
                k = me - distance * PAIR
                across(k, chunk).wait_recv()

                @pl.when(has_up)
                def _():
                    up(k, chunk).start()

                if chunk < EXTRA:

                    @pl.when(z != distance)
                    def _():
                        across(k, chunk).start()

                else:
                    across(k, chunk).start()

            @pl.when(z + distance < length)
            def _():
                k = me + distance * PAIR
                across(k, chunk).wait_recv()

                @pl.when(has_down)
                def _():
                    down(k, chunk).start()

                if chunk < EXTRA:

                    @pl.when(z + distance != last)
                    def _():
                        across(k, chunk).start()

                else:
                    across(k, chunk).start()

    def pass_ends(distance):
        for chunk in range(EXTRA):

            @pl.when(z == distance)
            def _():
                k = 1 - x
                across(k, chunk).wait_recv()

                @pl.when(has_up)
                def _():
                    up(k, chunk).start()

            if length > 1:

                @pl.when(z + distance == last)
                def _():
                    k = last * PAIR + 1 - x
                    across(k, chunk).wait_recv()

                    @pl.when(has_down)
                    def _():
                        down(k, chunk).start()

    def add_terms(distance):
        @pl.when(z - distance >= 0)
        def _():
            term(z - distance, False)

        @pl.when(z + distance < length)
        def _():
            term(z + distance, False)

    if length > 1:
        pass_line(1)
    pass_ends(0)
    term(z, True)

    @pl.loop(2, length)
    def steps(distance):
        pass_line(distance)
        pass_ends(distance - 1)
        add_terms(distance - 1)

    if length > 1:
        pass_ends(last)
        add_terms(last)

    lane = 128
    squares = product[...] * product[...]
    squares = jnp.sum(squares.reshape(squares.shape[0] // 8, 8, width), axis=0)
    mine = squares[:, :lane]
    for panel in range(1, width // lane):
        mine = mine + squares[:, panel * lane : (panel + 1) * lane]
    spot = me * cols + my_col
    parts[spot] = mine

    def part(slot, device):
        return pltpu.make_async_remote_copy(
            src_ref=parts.at[slot],
            dst_ref=parts.at[slot],
            send_sem=part_send.at[device],
            recv_sem=part_recv.at[slot],
            device_id={"blk": device // cols, "col": device % cols},
            device_id_type=MESH,
        )

    @pl.loop(1, total)
    def send_parts(step):
        part(spot, (spot + step) % total).start()

    @pl.loop(0, length)
    def sent(at):
        k = at * PAIR + x
        end = ((at == 0) | (at == last)) & (at != z)
        for chunk in range(CHUNKS):

            @pl.when(has_up & (at <= z))
            def _():
                up(k, chunk).wait_send()

            @pl.when(has_down & (at >= z))
            def _():
                down(k, chunk).wait_send()

            if chunk < EXTRA:

                @pl.when(jnp.logical_not(end))
                def _():
                    across(k, chunk).wait_send()

            else:
                across(k, chunk).wait_send()

    for chunk in range(EXTRA):

        @pl.when(has_up)
        def _():
            up(1 - x, chunk).wait_send()

        @pl.when(has_down)
        def _():
            down(last * PAIR + 1 - x, chunk).wait_send()

    @pl.loop(1, total)
    def get_parts(step):
        other = (spot + step) % total
        part(other, other).wait_recv()

    norm[0] = jnp.sum(jnp.sum(parts[...], axis=0))

    @pl.loop(1, total)
    def sent_parts(step):
        part(spot, (spot + step) % total).wait_send()


def solution(mesh):
    count = mesh.shape["blk"]
    cols = mesh.shape["col"]
    length = count // PAIR

    def per_device(
        density,
        occupied_p,
        hamil_dens,
        occupied_hp,
        window_sizes,
        row_window_sizes,
        slab_index,
        group_sizes,
    ):
        rows, inner = density.shape
        block, width = hamil_dens.shape
        hbm = pl.BlockSpec(memory_space=pltpu.HBM)
        vmem = pl.BlockSpec(memory_space=pltpu.VMEM)
        smem = pl.BlockSpec(memory_space=pltpu.SMEM)
        product, norm = pl.pallas_call(
            functools.partial(kernel, length, cols),
            out_shape=(
                pltpu.VMEM((rows, width), jnp.float32),
                jax.ShapeDtypeStruct((1,), jnp.float32),
            ),
            in_specs=[hbm] * 8,
            out_specs=(vmem, smem),
            scratch_shapes=[
                pltpu.VMEM((block, width), jnp.float32),
                pltpu.SMEM(occupied_p.shape, jnp.int32),
                pltpu.SMEM(occupied_hp.shape, jnp.int32),
                pltpu.SMEM(window_sizes.shape, jnp.int32),
                pltpu.SMEM(row_window_sizes.shape, jnp.int32),
                pltpu.SMEM(slab_index.shape, jnp.int32),
                pltpu.SMEM(group_sizes.shape, jnp.int32),
                pltpu.VMEM((count, block, width), jnp.float32),
                pltpu.VMEM((rows, inner), jnp.float32),
                pltpu.VMEM((length, rows, PAIR * block), jnp.bfloat16),
                pltpu.VMEM((length, rows, PAIR * block), jnp.bfloat16),
                pltpu.VMEM((count * cols, 8, 128), jnp.float32),
                pltpu.SemaphoreType.DMA((3, count, CHUNKS)),
                pltpu.SemaphoreType.DMA((count, CHUNKS)),
                pltpu.SemaphoreType.DMA((7 + CHUNKS,)),
                pltpu.SemaphoreType.DMA((count * cols,)),
                pltpu.SemaphoreType.DMA((count * cols,)),
            ],
            compiler_params=pltpu.CompilerParams(
                collective_id=0, has_side_effects=True, vmem_limit_bytes=56 << 20
            ),
        )(
            *(
                pltpu.with_memory_space_constraint(value, pltpu.HBM)
                for value in (
                    density,
                    hamil_dens,
                    occupied_p,
                    occupied_hp,
                    window_sizes,
                    row_window_sizes,
                    slab_index,
                    group_sizes,
                )
            )
        )
        return product, norm.reshape(())

    return jax.shard_map(
        per_device,
        mesh=mesh,
        in_specs=(
            P("blk", None),
            P("blk", None),
            P("blk", "col"),
            P("blk", "col"),
            P(),
            P(),
            P("col"),
            P(),
        ),
        out_specs=(P("blk", "col"), P()),
        check_vma=False,
    )
```

time: 42.6 us -> 38.3 us (0.90)
  Pallas kernels: 38.2 us -> 35 us
  local copies, waits for them, and re-layouts: 1.87 us -> 0.8 us
    pallas_call x1, Pallas kernels: 38.2 us -> 35 us  [per_device(): pl.pallas_call(functools.partial(kernel, length, cols), out_shape=(pltpu....]
    unnamed x1, local copies, waits for them, and re-layouts: 1.87 us -> 0.8 us
where the time goes in v1:
time: 38.3 us; the launch traced here: 38.2 us
  Pallas kernels  35 us (91%)
  between operations  2.33 us (6%)
  local copies, waits for them, and re-layouts  0.8 us (2%)
    pallas_call x1, Pallas kernels, per_device(): pl.pallas_call(functools.partial(kernel, length, cols), out_shape=(pltpu....  35 us
    unnamed x1, local copies, waits for them, and re-layouts  0.8 us

profile of v1, /device:TPU:0, one launch (start us, length us, event | category | flops | bytes accessed | tf_op | source)
XLA Modules:
  0.0 38.2 jit_solution(5009825176229689218)
XLA Ops:
  0.6 35.0 %shard_map.95 = (f32[256,512]{1,0:T(8,128)S(1)}, f32[1]{0:T(128)}) custom-call(f32[256,1024]{1,0:T(8,128)} %density.1, f32[128,512]{1,0:T(8,128)} %hamil_in.1, s32[2,8]{1,0:T(2,128)} %occ_p_in.1, s32[1,4]{1,0:T(1,128)} %occ_hp_in.1, s32[8]{0:T(128)} %window_in.1, s32[16]{0:T(128)} %row_window_in.1, s32[4]{0:T(128)} %slab_in.1, s32[782]{0:T(1024)} %groups_in.1), custom_call_target="tpu_custom_call" | custom-call | tf_op jit(solution)/shard_map/pallas_call | solution.py:372
  35.7 0.8 %copy.12 = f32[256,512]{1,0:T(8,128)} copy(f32[256,512]{1,0:T(8,128)S(1)} %get-tuple-element.6) | data formatting | bytes 1048576

commit v2 on v1

--- a/solution.py
+++ b/solution.py
@@ -111,11 +111,15 @@
         return pltpu.make_async_remote_copy(
             src_ref=rows,
             dst_ref=rows,
-            send_sem=send_sem.at[where, k, chunk],
+            send_sem=send_sem.at[where, k],
             recv_sem=recv_sem.at[k, chunk],
             device_id={"blk": device},
             device_id_type=MESH,
         )
+
+    def wait_sent(where, k, first, chunks):
+        rows = gathered.at[k, pl.ds(first * piece, chunks * piece), :]
+        pltpu.make_async_copy(rows, rows, send_sem.at[where, k]).wait()
 
     def up(k, chunk):
         return move(0, k, chunk, me + PAIR)
@@ -271,6 +275,19 @@
     pass_ends(0)
     term(z, True)
 
+    def half_term(at, side):
+        k = at * PAIR + side
+        if side is not x:
+            for chunk in range(EXTRA, CHUNKS):
+                across(k, chunk).wait_recv()
+        right = gathered[k]
+        high = right.astype(jnp.bfloat16)
+        low = (right - high.astype(jnp.float32)).astype(jnp.bfloat16)
+        here = pl.ds(pl.multiple_of(side * block, block), block)
+        left = p_high[at, :, here]
+        value = times(left, low) + times(p_low[at, :, here], high) + times(left, high)
+        product[...] = product[...] + value
+
     @pl.loop(2, length)
     def steps(distance):
         pass_line(distance)
@@ -278,8 +295,49 @@
         add_terms(distance - 1)
 
     if length > 1:
+        for end in (0, last):
+
+            @pl.when(z == last - end)
+            def _():
+                half_term(end, x)
+
         pass_ends(last)
-        add_terms(last)
+
+    @pl.loop(0, length)
+    def sent(at):
+        k = at * PAIR + x
+        end = ((at == 0) | (at == last)) & (at != z)
+
+        @pl.when(has_up & (at <= z))
+        def _():
+            wait_sent(0, k, 0, CHUNKS)
+
+        @pl.when(has_down & (at >= z))
+        def _():
+            wait_sent(1, k, 0, CHUNKS)
+
+        @pl.when(end)
+        def _():
+            wait_sent(2, k, EXTRA, CHUNKS - EXTRA)
+
+        @pl.when(jnp.logical_not(end))
+        def _():
+            wait_sent(2, k, 0, CHUNKS)
+
+    @pl.when(has_up)
+    def _():
+        wait_sent(0, 1 - x, 0, EXTRA)
+
+    @pl.when(has_down)
+    def _():
+        wait_sent(1, last * PAIR + 1 - x, 0, EXTRA)
+
+    if length > 1:
+        for end in (0, last):
+
+            @pl.when(z == last - end)
+            def _():
+                half_term(end, 1 - x)
 
     lane = 128
     squares = product[...] * product[...]
@@ -288,12 +346,12 @@
     for panel in range(1, width // lane):
         mine = mine + squares[:, panel * lane : (panel + 1) * lane]
     spot = me * cols + my_col
-    parts[spot] = mine
+    parts[spot, 0:1] = jnp.sum(mine, axis=0, keepdims=True)
 
     def part(slot, device):
         return pltpu.make_async_remote_copy(
-            src_ref=parts.at[slot],
-            dst_ref=parts.at[slot],
+            src_ref=parts.at[slot, pl.ds(0, 1)],
+            dst_ref=parts.at[slot, pl.ds(0, 1)],
             send_sem=part_send.at[device],
             recv_sem=part_recv.at[slot],
             device_id={"blk": device // cols, "col": device % cols},
@@ -304,45 +362,12 @@
     def send_parts(step):
         part(spot, (spot + step) % total).start()
 
-    @pl.loop(0, length)
-    def sent(at):
-        k = at * PAIR + x
-        end = ((at == 0) | (at == last)) & (at != z)
-        for chunk in range(CHUNKS):
-
-            @pl.when(has_up & (at <= z))
-            def _():
-                up(k, chunk).wait_send()
-
-            @pl.when(has_down & (at >= z))
-            def _():
-                down(k, chunk).wait_send()
-
-            if chunk < EXTRA:
-
-                @pl.when(jnp.logical_not(end))
-                def _():
-                    across(k, chunk).wait_send()
-
-            else:
-                across(k, chunk).wait_send()
-
-    for chunk in range(EXTRA):
-
-        @pl.when(has_up)
-        def _():
-            up(1 - x, chunk).wait_send()
-
-        @pl.when(has_down)
-        def _():
-            down(last * PAIR + 1 - x, chunk).wait_send()
-
     @pl.loop(1, total)
     def get_parts(step):
         other = (spot + step) % total
         part(other, other).wait_recv()
 
-    norm[0] = jnp.sum(jnp.sum(parts[...], axis=0))
+    norm[0] = jnp.sum(parts[:, 0, :])
 
     @pl.loop(1, total)
     def sent_parts(step):
@@ -390,7 +415,7 @@
                 pltpu.VMEM((length, rows, PAIR * block), jnp.bfloat16),
                 pltpu.VMEM((length, rows, PAIR * block), jnp.bfloat16),
                 pltpu.VMEM((count * cols, 8, 128), jnp.float32),
-                pltpu.SemaphoreType.DMA((3, count, CHUNKS)),
+                pltpu.SemaphoreType.DMA((3, count)),
                 pltpu.SemaphoreType.DMA((count, CHUNKS)),
                 pltpu.SemaphoreType.DMA((7 + CHUNKS,)),
                 pltpu.SemaphoreType.DMA((count * cols,)),

time: 38.3 us -> 36.6 us (0.956)
  Pallas kernels: 35 us -> 33.3 us
    pallas_call x1, Pallas kernels: 35 us -> 33.3 us  [per_device(): pl.pallas_call(functools.partial(kernel, length, cols), out_shape=(pltpu....]
where the time goes in v2:
time: 36.6 us; the launch traced here: 36.4 us
  Pallas kernels  33.3 us (91%)
  between operations  2.33 us (6%)
  local copies, waits for them, and re-layouts  0.8 us (2%)
    pallas_call x1, Pallas kernels, per_device(): pl.pallas_call(functools.partial(kernel, length, cols), out_shape=(pltpu....  33.3 us
    unnamed x1, local copies, waits for them, and re-layouts  0.8 us

profile of v2, /device:TPU:0, one launch (start us, length us, event | category | flops | bytes accessed | tf_op | source)
XLA Modules:
  0.0 36.4 jit_solution(9832388954699498460)
XLA Ops:
  0.6 33.3 %shard_map.95 = (f32[256,512]{1,0:T(8,128)S(1)}, f32[1]{0:T(128)}) custom-call(f32[256,1024]{1,0:T(8,128)} %density.1, f32[128,512]{1,0:T(8,128)} %hamil_in.1, s32[2,8]{1,0:T(2,128)} %occ_p_in.1, s32[1,4]{1,0:T(1,128)} %occ_hp_in.1, s32[8]{0:T(128)} %window_in.1, s32[16]{0:T(128)} %row_window_in.1, s32[4]{0:T(128)} %slab_in.1, s32[782]{0:T(1024)} %groups_in.1), custom_call_target="tpu_custom_call" | custom-call | tf_op jit(solution)/shard_map/pallas_call | solution.py:397
  34.0 0.8 %copy.12 = f32[256,512]{1,0:T(8,128)} copy(f32[256,512]{1,0:T(8,128)S(1)} %get-tuple-element.6) | data formatting | bytes 1048576

commit v3 on v1

--- a/solution.py
+++ b/solution.py
@@ -11,6 +11,7 @@
 PAIR = 2
 CHUNKS = 4
 EXTRA = 2
+HALF = 512
 
 
 def kernel(
@@ -111,11 +112,15 @@
         return pltpu.make_async_remote_copy(
             src_ref=rows,
             dst_ref=rows,
-            send_sem=send_sem.at[where, k, chunk],
+            send_sem=send_sem.at[where, k],
             recv_sem=recv_sem.at[k, chunk],
             device_id={"blk": device},
             device_id_type=MESH,
         )
+
+    def wait_sent(where, k, first, chunks):
+        rows = gathered.at[k, pl.ds(first * piece, chunks * piece), :]
+        pltpu.make_async_copy(rows, rows, send_sem.at[where, k]).wait()
 
     def up(k, chunk):
         return move(0, k, chunk, me + PAIR)
@@ -178,25 +183,10 @@
     def times(a, b):
         return jnp.dot(a, b, preferred_element_type=jnp.float32)
 
-    def term(at, first):
-        for chunk in range(CHUNKS):
-            if chunk < EXTRA:
-
-                @pl.when((at > 0) & (at < last))
-                def _():
-                    across(at * PAIR + 1 - x, chunk).wait_recv()
-
-            else:
-                across(at * PAIR + 1 - x, chunk).wait_recv()
-        right = gathered[pl.ds(at * PAIR, PAIR)].reshape(PAIR * block, width)
-        high = right.astype(jnp.bfloat16)
-        low = (right - high.astype(jnp.float32)).astype(jnp.bfloat16)
-        left = p_high[at]
-        value = times(left, low) + times(p_low[at], high) + times(left, high)
-        product[...] = value if first else product[...] + value
-
     def pass_line(distance):
-        for chunk in order:
+        @pl.loop(0, CHUNKS)
+        def each(step):
+            chunk = (step + EXTRA) % CHUNKS
 
             @pl.when(z - distance >= 0)
             def _():
@@ -207,13 +197,8 @@
                 def _():
                     up(k, chunk).start()
 
-                if chunk < EXTRA:
-
-                    @pl.when(z != distance)
-                    def _():
-                        across(k, chunk).start()
-
-                else:
+                @pl.when((z != distance) | (chunk >= EXTRA))
+                def _():
                     across(k, chunk).start()
 
             @pl.when(z + distance < length)
@@ -225,18 +210,13 @@
                 def _():
                     down(k, chunk).start()
 
-                if chunk < EXTRA:
-
-                    @pl.when(z + distance != last)
-                    def _():
-                        across(k, chunk).start()
-
-                else:
+                @pl.when((z + distance != last) | (chunk >= EXTRA))
+                def _():
                     across(k, chunk).start()
 
     def pass_ends(distance):
-        for chunk in range(EXTRA):
-
+        @pl.loop(0, EXTRA)
+        def each(chunk):
             @pl.when(z == distance)
             def _():
                 k = 1 - x
@@ -257,29 +237,74 @@
                     def _():
                         down(k, chunk).start()
 
+    def sends_done():
+        @pl.loop(0, length)
+        def sent(at):
+            k = at * PAIR + x
+            end = ((at == 0) | (at == last)) & (at != z)
+
+            @pl.when(has_up & (at <= z))
+            def _():
+                wait_sent(0, k, 0, CHUNKS)
+
+            @pl.when(has_down & (at >= z))
+            def _():
+                wait_sent(1, k, 0, CHUNKS)
+
+            @pl.when(end)
+            def _():
+                wait_sent(2, k, EXTRA, CHUNKS - EXTRA)
+
+            @pl.when(jnp.logical_not(end))
+            def _():
+                wait_sent(2, k, 0, CHUNKS)
+
+        @pl.when(has_up)
+        def _():
+            wait_sent(0, 1 - x, 0, EXTRA)
+
+        @pl.when(has_down)
+        def _():
+            wait_sent(1, last * PAIR + 1 - x, 0, EXTRA)
+
     def add_terms(distance):
-        @pl.when(z - distance >= 0)
-        def _():
-            term(z - distance, False)
-
-        @pl.when(z + distance < length)
-        def _():
-            term(z + distance, False)
-
-    if length > 1:
-        pass_line(1)
-    pass_ends(0)
-    term(z, True)
-
-    @pl.loop(2, length)
+        @pl.loop(0, 2)
+        def each(way):
+            at = z + (2 * way - 1) * distance
+
+            @pl.when((at >= 0) & (at < length) & ((distance > 0) | (way > 0)))
+            def _():
+                end = jnp.int32((at == 0) | (at == last))
+
+                @pl.loop(EXTRA * end, CHUNKS)
+                def wait(chunk):
+                    across(at * PAIR + 1 - x, chunk).wait_recv()
+
+                left_high = p_high[at]
+                left_low = p_low[at]
+
+                @pl.loop(0, width // half)
+                def columns(part):
+                    here = pl.ds(pl.multiple_of(part * half, half), half)
+                    right = gathered[pl.ds(at * PAIR, PAIR), :, here].reshape(PAIR * block, half)
+                    high = right.astype(jnp.bfloat16)
+                    low = (right - high.astype(jnp.float32)).astype(jnp.bfloat16)
+                    value = times(left_high, low) + times(left_low, high) + times(left_high, high)
+                    product[:, here] = product[:, here] + value
+
+    half = HALF
+    product[...] = jnp.zeros_like(product)
+
+    @pl.loop(1, length + 1)
     def steps(distance):
         pass_line(distance)
         pass_ends(distance - 1)
+
+        @pl.when(distance == length)
+        def _():
+            sends_done()
+
         add_terms(distance - 1)
-
-    if length > 1:
-        pass_ends(last)
-        add_terms(last)
 
     lane = 128
     squares = product[...] * product[...]
@@ -288,12 +313,12 @@
     for panel in range(1, width // lane):
         mine = mine + squares[:, panel * lane : (panel + 1) * lane]
     spot = me * cols + my_col
-    parts[spot] = mine
+    parts[spot, 0:1] = jnp.sum(mine, axis=0, keepdims=True)
 
     def part(slot, device):
         return pltpu.make_async_remote_copy(
-            src_ref=parts.at[slot],
-            dst_ref=parts.at[slot],
+            src_ref=parts.at[slot, pl.ds(0, 1)],
+            dst_ref=parts.at[slot, pl.ds(0, 1)],
             send_sem=part_send.at[device],
             recv_sem=part_recv.at[slot],
             device_id={"blk": device // cols, "col": device % cols},
@@ -304,49 +329,23 @@
     def send_parts(step):
         part(spot, (spot + step) % total).start()
 
-    @pl.loop(0, length)
-    def sent(at):
-        k = at * PAIR + x
-        end = ((at == 0) | (at == last)) & (at != z)
-        for chunk in range(CHUNKS):
-
-            @pl.when(has_up & (at <= z))
-            def _():
-                up(k, chunk).wait_send()
-
-            @pl.when(has_down & (at >= z))
-            def _():
-                down(k, chunk).wait_send()
-
-            if chunk < EXTRA:
-
-                @pl.when(jnp.logical_not(end))
-                def _():
-                    across(k, chunk).wait_send()
-
-            else:
-                across(k, chunk).wait_send()
-
-    for chunk in range(EXTRA):
-
-        @pl.when(has_up)
-        def _():
-            up(1 - x, chunk).wait_send()
-
-        @pl.when(has_down)
-        def _():
-            down(last * PAIR + 1 - x, chunk).wait_send()
-
     @pl.loop(1, total)
     def get_parts(step):
         other = (spot + step) % total
         part(other, other).wait_recv()
 
-    norm[0] = jnp.sum(jnp.sum(parts[...], axis=0))
+    norm[0] = jnp.sum(parts[:, 0, :])
 
     @pl.loop(1, total)
     def sent_parts(step):
         part(spot, (spot + step) % total).wait_send()
+
+
+def finish(product_in, norm_in, product_out, norm_out, sem):
+    store = pltpu.make_async_copy(product_in, product_out, sem)
+    store.start()
+    norm_out[0] = norm_in[0]
+    store.wait()
 
 
 def solution(mesh):
@@ -390,7 +389,7 @@
                 pltpu.VMEM((length, rows, PAIR * block), jnp.bfloat16),
                 pltpu.VMEM((length, rows, PAIR * block), jnp.bfloat16),
                 pltpu.VMEM((count * cols, 8, 128), jnp.float32),
-                pltpu.SemaphoreType.DMA((3, count, CHUNKS)),
+                pltpu.SemaphoreType.DMA((3, count)),
                 pltpu.SemaphoreType.DMA((count, CHUNKS)),
                 pltpu.SemaphoreType.DMA((7 + CHUNKS,)),
                 pltpu.SemaphoreType.DMA((count * cols,)),
@@ -414,6 +413,17 @@
                 )
             )
         )
+        product, norm = pl.pallas_call(
+            finish,
+            out_shape=(
+                jax.ShapeDtypeStruct((rows, width), jnp.float32),
+                jax.ShapeDtypeStruct((1,), jnp.float32),
+            ),
+            in_specs=[vmem, smem],
+            out_specs=(hbm, smem),
+            scratch_shapes=[pltpu.SemaphoreType.DMA(())],
+            compiler_params=pltpu.CompilerParams(vmem_limit_bytes=1 << 20),
+        )(pltpu.with_memory_space_constraint(product, pltpu.VMEM), norm)
         return product, norm.reshape(())
 
     return jax.shard_map(

time: 38.3 us -> 36.1 us (0.943)
  between operations: 2.33 us -> 0.64 us
  local copies, waits for them, and re-layouts: 0.8 us -> 0 us
    pallas_call x0 -> x1, Pallas kernels: none -> 1.95 us  [per_device(): pl.pallas_call(finish, out_shape=(jax.ShapeDtypeStruct((rows, width), jnp...]
    pallas_call x1, Pallas kernels: 35 us -> 33.4 us  [per_device(): pl.pallas_call(functools.partial(kernel, length, cols), out_shape=(pltpu....]
    unnamed x1 -> x0, local copies, waits for them, and re-layouts: 0.8 us -> none
where the time goes in v3:
time: 36.1 us; the launch traced here: 36 us
  Pallas kernels  35.3 us (98%)
  between operations  0.64 us (2%)
    pallas_call x1, Pallas kernels, per_device(): pl.pallas_call(functools.partial(kernel, length, cols), out_shape=(pltpu....  33.4 us
    pallas_call x1, Pallas kernels, per_device(): pl.pallas_call(finish, out_shape=(jax.ShapeDtypeStruct((rows, width), jnp...  1.95 us

profile of v3, /device:TPU:0, one launch (start us, length us, event | category | flops | bytes accessed | tf_op | source)
XLA Modules:
  0.0 36.0 jit_solution(2537444962978272435)
XLA Ops:
  0.6 33.4 %shard_map.95 = (f32[256,512]{1,0:T(8,128)S(1)}, f32[1]{0:T(128)}) custom-call(f32[256,1024]{1,0:T(8,128)} %density.1, f32[128,512]{1,0:T(8,128)} %hamil_in.1, s32[2,8]{1,0:T(2,128)} %occ_p_in.1, s32[1,4]{1,0:T(1,128)} %occ_hp_in.1, s32[8]{0:T(128)} %window_in.1, s32[16]{0:T(128)} %row_window_in.1, s32[4]{0:T(128)} %slab_in.1, s32[782]{0:T(1024)} %groups_in.1), custom_call_target="tpu_custom_call" | custom-call | tf_op jit(solution)/shard_map/pallas_call | solution.py:371
  34.0 2.0 %shard_map.96 = (f32[256,512]{1,0:T(8,128)}, f32[1]{0:T(128)}) custom-call(f32[256,512]{1,0:T(8,128)S(1)} %get-tuple-element.6.product_in, f32[1]{0:T(128)} %get-tuple-element.7.norm_in), custom_call_target="tpu_custom_call" | custom-call | tf_op jit(solution)/shard_map/pallas_call | solution.py:416

commit v4 on v3

--- a/solution.py
+++ b/solution.py
@@ -334,18 +334,21 @@
         other = (spot + step) % total
         part(other, other).wait_recv()
 
-    norm[0] = jnp.sum(parts[:, 0, :])
+    norm[...] = jnp.sum(parts[:, 0, :], axis=0, keepdims=True)
 
     @pl.loop(1, total)
     def sent_parts(step):
         part(spot, (spot + step) % total).wait_send()
 
 
-def finish(product_in, norm_in, product_out, norm_out, sem):
-    store = pltpu.make_async_copy(product_in, product_out, sem)
+def finish(product_in, norm_in, product_out, norm_out, value, sem):
+    store = pltpu.make_async_copy(product_in, product_out, sem.at[0])
     store.start()
-    norm_out[0] = norm_in[0]
+    value[0] = jnp.sum(norm_in[...])
+    send = pltpu.make_async_copy(value, norm_out, sem.at[1])
+    send.start()
     store.wait()
+    send.wait()
 
 
 def solution(mesh):
@@ -372,10 +375,10 @@
             functools.partial(kernel, length, cols),
             out_shape=(
                 pltpu.VMEM((rows, width), jnp.float32),
-                jax.ShapeDtypeStruct((1,), jnp.float32),
+                pltpu.VMEM((1, 128), jnp.float32),
             ),
             in_specs=[hbm] * 8,
-            out_specs=(vmem, smem),
+            out_specs=(vmem, vmem),
             scratch_shapes=[
                 pltpu.VMEM((block, width), jnp.float32),
                 pltpu.SMEM(occupied_p.shape, jnp.int32),
@@ -419,11 +422,11 @@
                 jax.ShapeDtypeStruct((rows, width), jnp.float32),
                 jax.ShapeDtypeStruct((1,), jnp.float32),
             ),
-            in_specs=[vmem, smem],
-            out_specs=(hbm, smem),
-            scratch_shapes=[pltpu.SemaphoreType.DMA(())],
+            in_specs=[vmem, vmem],
+            out_specs=(hbm, hbm),
+            scratch_shapes=[pltpu.SMEM((1,), jnp.float32), pltpu.SemaphoreType.DMA((2,))],
             compiler_params=pltpu.CompilerParams(vmem_limit_bytes=1 << 20),
-        )(pltpu.with_memory_space_constraint(product, pltpu.VMEM), norm)
+        )(pltpu.with_memory_space_constraint(product, pltpu.VMEM), pltpu.with_memory_space_constraint(norm, pltpu.VMEM))
         return product, norm.reshape(())
 
     return jax.shard_map(

time: 36.1 us -> 34.4 us (0.953)
  Pallas kernels: 35.3 us -> 33.6 us
    pallas_call x1, Pallas kernels: 1.95 us -> 0.82 us  [per_device(): pl.pallas_call(finish, out_shape=(jax.ShapeDtypeStruct((rows, width), jnp...]
    pallas_call x1, Pallas kernels: 33.4 us -> 32.7 us  [per_device(): pl.pallas_call(functools.partial(kernel, length, cols), out_shape=(pltpu....]
where the time goes in v4:
time: 34.4 us; the launch traced here: 34.2 us
  Pallas kernels  33.6 us (98%)
  between operations  0.64 us (2%)
    pallas_call x1, Pallas kernels, per_device(): pl.pallas_call(functools.partial(kernel, length, cols), out_shape=(pltpu....  32.7 us
    pallas_call x1, Pallas kernels, per_device(): pl.pallas_call(finish, out_shape=(jax.ShapeDtypeStruct((rows, width), jnp...  0.82 us

profile of v4, /device:TPU:0, one launch (start us, length us, event | category | flops | bytes accessed | tf_op | source)
XLA Modules:
  0.0 34.2 jit_solution(8142994153149151747)
XLA Ops:
  0.6 32.7 %shard_map.95 = (f32[256,512]{1,0:T(8,128)S(1)}, f32[1,128]{1,0:T(1,128)S(1)}) custom-call(f32[256,1024]{1,0:T(8,128)} %density.1, f32[128,512]{1,0:T(8,128)} %hamil_in.1, s32[2,8]{1,0:T(2,128)} %occ_p_in.1, s32[1,4]{1,0:T(1,128)} %occ_hp_in.1, s32[8]{0:T(128)} %window_in.1, s32[16]{0:T(128)} %row_window_in.1, s32[4]{0:T(128)} %slab_in.1, s32[782]{0:T(1024)} %groups_in.1), custom_call_target="tpu_custom_call" | custom-call | tf_op jit(solution)/shard_map/pallas_call | solution.py:374
  33.4 0.8 %shard_map.96 = (f32[256,512]{1,0:T(8,128)}, f32[1]{0:T(128)}) custom-call(f32[256,512]{1,0:T(8,128)S(1)} %get-tuple-element.6.product_in, f32[1,128]{1,0:T(1,128)S(1)} %get-tuple-element.7.norm_in), custom_call_target="tpu_custom_call" | custom-call | tf_op jit(solution)/shard_map/pallas_call | solution.py:419

commit v5 on v4

v5 whole, which is shorter than its diff:
```python
import functools

import jax
import jax.numpy as jnp
from jax import lax
from jax.experimental import pallas as pl
from jax.experimental.pallas import tpu as pltpu
from jax.sharding import PartitionSpec as P

MESH = pl.DeviceIdType.MESH
PAIR = 2
EXTRA = 2
TOP_EXTRA = 1
NEAR = 2
CORES = 2
FAR_AFTER = 1


def kernel(
    length,
    cols,
    density,
    hamil_in,
    occ_p_in,
    occ_hp_in,
    window_in,
    row_window_in,
    slab_in,
    groups_in,
    product,
    norm,
    hamil,
    occ_p,
    occ_hp,
    window,
    row_window,
    slab,
    groups,
    gathered,
    p_in,
    p_high,
    p_low,
    p_far,
    far_part,
    parts,
    send_sem,
    recv_sem,
    load_sem,
    part_send,
    part_recv,
    far_send,
    far_recv,
    far_sem,
):
    count = length * PAIR
    total = count * cols
    block, width = hamil.shape
    row_blocks = product.shape[0] // block
    panels = width // block
    far = length >= NEAR + 2
    me = lax.axis_index("blk")
    my_col = lax.axis_index("col")
    z = me // PAIR
    x = me % PAIR
    partner = me + 1 - 2 * x
    last = length - 1
    has_up = z < last
    has_down = z > 0
    is_last = z == last
    is_near = z == last - 1

    loads = [
        pltpu.make_async_copy(source, target, load_sem.at[at])
        for at, (source, target) in enumerate(
            (
                (occ_hp_in, occ_hp),
                (window_in, window),
                (slab_in, slab),
                (groups_in, groups),
                (row_window_in, row_window),
                (occ_p_in, occ_p),
                (density, p_in),
            )
        )
    ]
    hamil_loads = [
        pltpu.make_async_copy(
            hamil_in.at[:, pl.ds(panel * block, block)],
            hamil.at[:, pl.ds(panel * block, block)],
            load_sem.at[len(loads) + panel],
        )
        for panel in range(panels)
    ]
    barrier = pltpu.get_barrier_semaphore()

    def greet(device):
        pl.semaphore_signal(barrier, inc=1, device_id=device, device_id_type=MESH)

    greet({"blk": partner})

    @pl.when(has_up)
    def _():
        greet({"blk": me + PAIR})

    @pl.when(has_down)
    def _():
        greet({"blk": me - PAIR})

    @pl.loop(1, cols)
    def greet_col(step):
        greet({"col": (my_col + step) % cols})

    for load in loads[:4] + hamil_loads + loads[4:]:
        load.start()

    for load in loads[:4]:
        load.wait()

    def move(where, k, panel, device):
        spot = gathered.at[k, panel]
        return pltpu.make_async_remote_copy(
            src_ref=spot,
            dst_ref=spot,
            send_sem=send_sem.at[where, k],
            recv_sem=recv_sem.at[k, panel],
            device_id={"blk": device},
            device_id_type=MESH,
        )

    def wait_sent(where, k, first, amount):
        spot = gathered.at[k, pl.ds(first, amount)]
        pltpu.make_async_copy(spot, spot, send_sem.at[where, k]).wait()

    def up(k, panel):
        return move(0, k, panel, me + PAIR)

    def down(k, panel):
        return move(1, k, panel, me - PAIR)

    def across(k, panel):
        return move(2, k, panel, partner)

    share = product.shape[0] // cols
    pair = PAIR * block

    mate = my_col + 1 - CORES * (my_col % CORES)

    def far_move(who, plane, device, sem, onward=0):
        spot = p_far.at[pl.ds(pl.multiple_of(who * share, share), share), pl.ds(plane * pair, pair)]
        return pltpu.make_async_remote_copy(
            src_ref=spot,
            dst_ref=spot,
            send_sem=far_send.at[onward, sem, plane],
            recv_sem=far_recv.at[who, plane],
            device_id=device,
            device_id_type=MESH,
        )

    def far_down(plane):
        return far_move(my_col, plane, {"blk": me - PAIR}, my_col)

    def far_to(peer, plane):
        return far_move(my_col, plane, {"col": peer}, peer)

    def far_result():
        return pltpu.make_async_remote_copy(
            src_ref=far_part,
            dst_ref=far_part,
            send_sem=far_sem.at[0],
            recv_sem=far_sem.at[1],
            device_id={"blk": me + PAIR},
            device_id_type=MESH,
        )

    row_at = lax.broadcasted_iota(jnp.int32, (block, block), 0)
    col_at = lax.broadcasted_iota(jnp.int32, (block, block), 1)

    def send_far():
        for load in loads[4:]:
            load.wait()
        first = my_col * share
        b = first // block
        share_row = lax.broadcasted_iota(jnp.int32, (share, block), 0) + first - b * block
        share_col = lax.broadcasted_iota(jnp.int32, (share, block), 1)
        rows = pl.ds(pl.multiple_of(first, share), share)
        live = share_row < row_window[me * row_blocks + b]
        for plane in range(NEAR):
            for other in range(PAIR):
                k = (last - NEAR + plane) * PAIR + other
                mask = jnp.where(
                    live & (share_col < window[k]), occ_p[b, k].astype(jnp.float32), 0.0
                )
                p_far[rows, pl.ds(plane * pair + other * block, block)] = (
                    p_in[rows, pl.ds(k * block, block)] * mask
                )
            far_down(plane).start()
        for plane in range(NEAR):
            for other in range(PAIR):
                k = (last - NEAR + plane) * PAIR + other
                gathered[k, 0] = jnp.zeros((block, block), jnp.float32)

    rows_live = row_at < window[me]
    for panel in range(panels):
        hamil_loads[panel].wait()
        size = groups[slab[panel]]
        occupied = occ_hp[0, panel].astype(jnp.float32)
        mask = jnp.where(rows_live & (col_at < size), occupied, 0.0)
        gathered[me, panel] = hamil[:, panel * block : (panel + 1) * block] * mask
        if panel == 0:
            ends = jnp.int32(z == 0) + jnp.int32(z == last)
            pl.semaphore_wait(barrier, PAIR - 1 + cols - 1 + 2 - ends)

        across(me, panel).start()
        if panel == 0 and far:

            @pl.when(has_up & jnp.logical_not(is_near))
            def _():
                up(me, panel).start()

        else:

            @pl.when(has_up)
            def _():
                up(me, panel).start()

        @pl.when(has_down)
        def _():
            down(me, panel).start()

        if panel == FAR_AFTER and far:
            pl.when(is_last)(send_far)

    def wait_loads():
        for load in loads[4:]:
            load.wait()

    if far:
        pl.when(jnp.logical_not(is_last))(wait_loads)
    else:
        wait_loads()

    @pl.loop(0, length)
    def split(at):
        for b in range(row_blocks):
            live = row_at < row_window[me * row_blocks + b]
            here = pl.ds(b * block, block)
            for other in range(PAIR):
                k = at * PAIR + other
                mask = jnp.where(
                    live & (col_at < window[k]), occ_p[b, k].astype(jnp.float32), 0.0
                )
                value = p_in[here, pl.ds(pl.multiple_of(k * block, block), block)] * mask
                high = value.astype(jnp.bfloat16)
                there = pl.ds(other * block, block)
                p_high[at, here, there] = high
                p_low[at, here, there] = (value - high.astype(jnp.float32)).astype(jnp.bfloat16)

    def times(a, b):
        return jnp.dot(a, b, preferred_element_type=jnp.float32)

    def first_panel(at):
        if not far:
            return 0
        return jnp.int32(is_last & (at >= last - NEAR) & (at < last))

    def end_panel(at):
        low = (at == 0) & (z > 0)
        high = (at == last) & (z < last)
        top = low & is_last
        return panels - EXTRA * jnp.int32(low | high) + (EXTRA - TOP_EXTRA) * jnp.int32(top)

    def pass_below(distance, panel):
        at = z - distance

        @pl.when((at >= 0) & (distance > 0) & (panel >= first_panel(at)))
        def _():
            k = me - distance * PAIR
            across(k, panel).wait_recv()
            skip = (panel == 0) & is_near & (at >= last - NEAR) if far else False

            @pl.when(has_up & jnp.logical_not(skip))
            def _():
                up(k, panel).start()

            @pl.when(panel < end_panel(at))
            def _():
                across(k, panel).start()

    def pass_above(distance, panel):
        at = z + distance

        @pl.when((at < length) & (distance > 0))
        def _():
            k = me + distance * PAIR
            across(k, panel).wait_recv()

            @pl.when(has_down)
            def _():
                down(k, panel).start()

            @pl.when(panel < end_panel(at))
            def _():
                across(k, panel).start()

    def pass_low_end(distance):
        @pl.when((z == distance) & has_up)
        def _():
            for panel in range(panels - EXTRA, panels):
                k = 1 - x
                across(k, panel).wait_recv()
                if panel >= panels - TOP_EXTRA:
                    up(k, panel).start()
                else:

                    @pl.when(jnp.logical_not(is_near))
                    def _():
                        up(k, panel).start()

    def pass_high_end(distance):
        @pl.when((z + distance == last) & has_down)
        def _():
            for panel in range(panels - EXTRA, panels):
                k = last * PAIR + 1 - x
                across(k, panel).wait_recv()
                down(k, panel).start()

    def sends_done():
        @pl.loop(0, length)
        def sent(at):
            k = at * PAIR + x

            @pl.when(has_down & (at >= z))
            def _():
                wait_sent(1, k, 0, panels)

            short = is_near & (at >= last - NEAR) if far else False

            @pl.when(has_up & (at <= z) & jnp.logical_not(short))
            def _():
                wait_sent(0, k, 0, panels)

            @pl.when(has_up & (at <= z) & short)
            def _():
                wait_sent(0, k, 1, panels - 1)

            amount = end_panel(at) - first_panel(at)
            for size in sorted({panels, panels - 1, panels - EXTRA, panels - TOP_EXTRA}):

                @pl.when(amount == size)
                def _():
                    wait_sent(2, k, 0, size)

        @pl.when(has_up & is_near)
        def _():
            wait_sent(0, 1 - x, 0, TOP_EXTRA)

        @pl.when(has_up & jnp.logical_not(is_near))
        def _():
            wait_sent(0, 1 - x, 0, EXTRA)

        @pl.when(has_down)
        def _():
            wait_sent(1, last * PAIR + 1 - x, 0, EXTRA)

        if far:

            @pl.when(is_last)
            def _():
                for plane in range(NEAR):
                    far_down(plane).wait_send()

            @pl.when(is_near)
            def _():
                @pl.loop(1, cols // CORES)
                def peers(step):
                    who = (my_col + step * CORES) % cols
                    for plane in range(NEAR):
                        far_to(who, plane).wait_send()
                        far_move(who, plane, {"col": mate}, who, 1).wait_send()

                for plane in range(NEAR):
                    far_to(mate, plane).wait_send()

                far_result().wait_send()

    def split_in_two(value):
        high = value.astype(jnp.bfloat16)
        return high, (value - high.astype(jnp.float32)).astype(jnp.bfloat16)

    def right_of(at, panel):
        return gathered[pl.ds(at * PAIR, PAIR), panel].reshape(pair, block)

    def add_terms(distance):
        @pl.loop(0, 2)
        def each(way):
            at = z + (2 * way - 1) * distance

            @pl.when((at >= 0) & (at < length) & ((distance > 0) | ((distance == 0) & (way > 0))))
            def _():
                passed = ((at == 0) & has_up) | ((at == last) & has_down)

                first = first_panel(at)
                if far:
                    first = first + jnp.int32(is_near & (at >= last - NEAR) & (at < last))

                @pl.loop(first, panels - EXTRA * jnp.int32(passed))
                def wait(panel):
                    across(at * PAIR + 1 - x, panel).wait_recv()

                if far:

                    @pl.when(is_last & (distance == last))
                    def _():
                        far_result().wait_recv()

                left_high = p_high[at]
                left_low = p_low[at]
                right = jnp.concatenate([right_of(at, panel) for panel in range(panels)], axis=1)
                high, low = split_in_two(right)
                value = times(left_high, low) + times(left_low, high) + times(left_high, high)
                product[...] = product[...] + value

    def forward_far(plane):
        far_to(mate, plane).wait_recv()

        @pl.loop(1, cols // CORES)
        def peers(step):
            far_to((my_col + step * CORES) % cols, plane).start()

        far_to(mate, plane).start()

    def mate_far(plane):
        @pl.loop(1, cols // CORES)
        def peers(step):
            who = (my_col + step * CORES) % cols
            far_move(who, plane, {"col": mate}, who, 1).wait_recv()
            far_move(who, plane, {"col": mate}, who, 1).start()

    def give_far():
        @pl.loop(0, cols // CORES)
        def mates(step):
            who = (mate + step * CORES) % cols
            for plane in range(NEAR):
                far_move(who, plane, {"col": mate}, who).wait_recv()

        value = None
        for plane in range(NEAR):
            at = last - NEAR + plane
            across(at * PAIR + 1 - x, 0).wait_recv()
            left_high, left_low = split_in_two(p_far[:, plane * pair : (plane + 1) * pair])
            high, low = split_in_two(right_of(at, 0))
            one = times(left_high, low) + times(left_low, high) + times(left_high, high)
            value = one if value is None else value + one
        far_part[...] = value
        far_result().start()

    product[...] = jnp.zeros_like(product)
    inner = jnp.int32((z > 0) & (z < last))

    @pl.loop(0, length + 2)
    def steps(distance):
        @pl.loop(0, panels)
        def lines(panel):
            pass_below(distance + 1, panel)
            ahead = distance * panels + panel + panels // 2
            pass_above(ahead // panels, ahead % panels)

        if far:

            @pl.when(is_near & (distance == 0))
            def _():
                for plane in range(NEAR):
                    forward_far(plane)

            @pl.when(is_near & (distance == 1))
            def _():
                for plane in range(NEAR):
                    mate_far(plane)

        pass_low_end(distance)
        pass_high_end(distance)
        if far:

            @pl.when(is_near & (distance == 1))
            def _():
                give_far()

        @pl.when(distance == length)
        def _():
            sends_done()

        add_terms(distance - 1 - inner)

    if far:

        @pl.when(is_last)
        def _():
            product[:, 0:block] = product[:, 0:block] + far_part[...]

    lane = 128
    squares = product[...] * product[...]
    squares = jnp.sum(squares.reshape(squares.shape[0] // 8, 8, width), axis=0)
    mine = squares[:, :lane]
    for panel in range(1, width // lane):
        mine = mine + squares[:, panel * lane : (panel + 1) * lane]
    spot = me * cols + my_col
    parts[spot, 0:1] = jnp.sum(mine, axis=0, keepdims=True)

    def part(slot, device):
        return pltpu.make_async_remote_copy(
            src_ref=parts.at[slot, pl.ds(0, 1)],
            dst_ref=parts.at[slot, pl.ds(0, 1)],
            send_sem=part_send.at[device],
            recv_sem=part_recv.at[slot],
            device_id={"blk": device // cols, "col": device % cols},
            device_id_type=MESH,
        )

    @pl.loop(0, total)
    def send_parts(device):
        @pl.when(device != spot)
        def _():
            part(spot, device).start()

    @pl.loop(1, total)
    def get_parts(step):
        other = (spot + step) % total
        part(other, other).wait_recv()

    norm[...] = jnp.sum(parts[:, 0, :], axis=0, keepdims=True)

    @pl.loop(1, total)
    def sent_parts(step):
        part(spot, (spot + step) % total).wait_send()


def finish(product_in, norm_in, product_out, norm_out, value, sem):
    store = pltpu.make_async_copy(product_in, product_out, sem.at[0])
    store.start()
    value[0] = jnp.sum(norm_in[...])
    send = pltpu.make_async_copy(value, norm_out, sem.at[1])
    send.start()
    store.wait()
    send.wait()


def solution(mesh):
    count = mesh.shape["blk"]
    cols = mesh.shape["col"]
    length = count // PAIR

    def per_device(
        density,
        occupied_p,
        hamil_dens,
        occupied_hp,
        window_sizes,
        row_window_sizes,
        slab_index,
        group_sizes,
    ):
        rows, inner = density.shape
        block, width = hamil_dens.shape
        hbm = pl.BlockSpec(memory_space=pltpu.HBM)
        vmem = pl.BlockSpec(memory_space=pltpu.VMEM)
        smem = pl.BlockSpec(memory_space=pltpu.SMEM)
        product, norm = pl.pallas_call(
            functools.partial(kernel, length, cols),
            out_shape=(
                pltpu.VMEM((rows, width), jnp.float32),
                pltpu.VMEM((1, 128), jnp.float32),
            ),
            in_specs=[hbm] * 8,
            out_specs=(vmem, vmem),
            scratch_shapes=[
                pltpu.VMEM((block, width), jnp.float32),
                pltpu.SMEM(occupied_p.shape, jnp.int32),
                pltpu.SMEM(occupied_hp.shape, jnp.int32),
                pltpu.SMEM(window_sizes.shape, jnp.int32),
                pltpu.SMEM(row_window_sizes.shape, jnp.int32),
                pltpu.SMEM(slab_index.shape, jnp.int32),
                pltpu.SMEM(group_sizes.shape, jnp.int32),
                pltpu.VMEM((count, width // block, block, block), jnp.float32),
                pltpu.VMEM((rows, inner), jnp.float32),
                pltpu.VMEM((length, rows, PAIR * block), jnp.bfloat16),
                pltpu.VMEM((length, rows, PAIR * block), jnp.bfloat16),
                pltpu.VMEM((rows, NEAR * PAIR * block), jnp.float32),
                pltpu.VMEM((rows, block), jnp.float32),
                pltpu.VMEM((count * cols, 8, 128), jnp.float32),
                pltpu.SemaphoreType.DMA((3, count)),
                pltpu.SemaphoreType.DMA((count, width // block)),
                pltpu.SemaphoreType.DMA((7 + width // block,)),
                pltpu.SemaphoreType.DMA((count * cols,)),
                pltpu.SemaphoreType.DMA((count * cols,)),
                pltpu.SemaphoreType.DMA((2, cols, NEAR)),
                pltpu.SemaphoreType.DMA((cols, NEAR)),
                pltpu.SemaphoreType.DMA((2,)),
            ],
            compiler_params=pltpu.CompilerParams(
                collective_id=0, has_side_effects=True, vmem_limit_bytes=56 << 20
            ),
        )(
            *(
                pltpu.with_memory_space_constraint(value, pltpu.HBM)
                for value in (
                    density,
                    hamil_dens,
                    occupied_p,
                    occupied_hp,
                    window_sizes,
                    row_window_sizes,
                    slab_index,
                    group_sizes,
                )
            )
        )
        product, norm = pl.pallas_call(
            finish,
            out_shape=(
                jax.ShapeDtypeStruct((rows, width), jnp.float32),
                jax.ShapeDtypeStruct((1,), jnp.float32),
            ),
            in_specs=[vmem, vmem],
            out_specs=(hbm, hbm),
            scratch_shapes=[pltpu.SMEM((1,), jnp.float32), pltpu.SemaphoreType.DMA((2,))],
            compiler_params=pltpu.CompilerParams(vmem_limit_bytes=1 << 20),
        )(pltpu.with_memory_space_constraint(product, pltpu.VMEM), pltpu.with_memory_space_constraint(norm, pltpu.VMEM))
        return product, norm.reshape(())

    return jax.shard_map(
        per_device,
        mesh=mesh,
        in_specs=(
            P("blk", None),
            P("blk", None),
            P("blk", "col"),
            P("blk", "col"),
            P(),
            P(),
            P("col"),
            P(),
        ),
        out_specs=(P("blk", "col"), P()),
        check_vma=False,
    )
```

time: 34.4 us -> 33.9 us (0.985)
  Pallas kernels: 33.6 us -> 33.1 us
    pallas_call x1, Pallas kernels: 32.7 us -> 32.3 us  [per_device(): pl.pallas_call(functools.partial(kernel, length, cols), out_shape=(pltpu....]
where the time goes in v5:
time: 33.9 us; the launch traced here: 33.8 us
  Pallas kernels  33.1 us (98%)
  between operations  0.64 us (2%)
    pallas_call x1, Pallas kernels, per_device(): pl.pallas_call(functools.partial(kernel, length, cols), out_shape=(pltpu....  32.3 us
    pallas_call x1, Pallas kernels, per_device(): pl.pallas_call(finish, out_shape=(jax.ShapeDtypeStruct((rows, width), jnp...  0.82 us

profile of v5, /device:TPU:0, one launch (start us, length us, event | category | flops | bytes accessed | tf_op | source)
XLA Modules:
  0.0 33.8 jit_solution(6315786521502935651)
XLA Ops:
  0.6 32.3 %shard_map.95 = (f32[256,512]{1,0:T(8,128)S(1)}, f32[1,128]{1,0:T(1,128)S(1)}) custom-call(f32[256,1024]{1,0:T(8,128)} %density.1, f32[128,512]{1,0:T(8,128)} %hamil_in.1, s32[2,8]{1,0:T(2,128)} %occ_p_in.1, s32[1,4]{1,0:T(1,128)} %occ_hp_in.1, s32[8]{0:T(128)} %window_in.1, s32[16]{0:T(128)} %row_window_in.1, s32[4]{0:T(128)} %slab_in.1, s32[782]{0:T(1024)} %groups_in.1), custom_call_target="tpu_custom_call" | custom-call | tf_op jit(solution)/shard_map/pallas_call | solution.py:567
  32.9 0.8 %shard_map.96 = (f32[256,512]{1,0:T(8,128)}, f32[1]{0:T(128)}) custom-call(f32[256,512]{1,0:T(8,128)S(1)} %get-tuple-element.6.product_in, f32[1,128]{1,0:T(1,128)S(1)} %get-tuple-element.7.norm_in), custom_call_target="tpu_custom_call" | custom-call | tf_op jit(solution)/shard_map/pallas_call | solution.py:617

commit v6 on v5

--- a/solution.py
+++ b/solution.py
@@ -13,6 +13,7 @@
 TOP_EXTRA = 1
 NEAR = 2
 CORES = 2
+GROUP = 2
 FAR_AFTER = 1
 
 
@@ -46,8 +47,7 @@
     send_sem,
     recv_sem,
     load_sem,
-    part_send,
-    part_recv,
+    part_sem,
     far_send,
     far_recv,
     far_sem,
@@ -403,22 +403,29 @@
                 if far:
                     first = first + jnp.int32(is_near & (at >= last - NEAR) & (at < last))
 
-                @pl.loop(first, panels - EXTRA * jnp.int32(passed))
-                def wait(panel):
-                    across(at * PAIR + 1 - x, panel).wait_recv()
+                limit = panels - EXTRA * jnp.int32(passed)
+                left_high = p_high[at]
+                left_low = p_low[at]
+                for begin in range(0, panels, GROUP):
+                    for panel in range(begin, begin + GROUP):
+
+                        @pl.when((panel >= first) & (panel < limit))
+                        def _():
+                            across(at * PAIR + 1 - x, panel).wait_recv()
+
+                    right = jnp.concatenate(
+                        [right_of(at, begin + panel) for panel in range(GROUP)], axis=1
+                    )
+                    high, low = split_in_two(right)
+                    value = times(left_high, low) + times(left_low, high) + times(left_high, high)
+                    here = slice(begin * block, (begin + GROUP) * block)
+                    product[:, here] = product[:, here] + value
 
                 if far:
 
                     @pl.when(is_last & (distance == last))
                     def _():
                         far_result().wait_recv()
-
-                left_high = p_high[at]
-                left_low = p_low[at]
-                right = jnp.concatenate([right_of(at, panel) for panel in range(panels)], axis=1)
-                high, low = split_in_two(right)
-                value = times(left_high, low) + times(left_low, high) + times(left_high, high)
-                product[...] = product[...] + value
 
     def forward_far(plane):
         far_to(mate, plane).wait_recv()
@@ -510,8 +517,8 @@
         return pltpu.make_async_remote_copy(
             src_ref=parts.at[slot, pl.ds(0, 1)],
             dst_ref=parts.at[slot, pl.ds(0, 1)],
-            send_sem=part_send.at[device],
-            recv_sem=part_recv.at[slot],
+            send_sem=part_sem.at[0],
+            recv_sem=part_sem.at[1],
             device_id={"blk": device // cols, "col": device % cols},
             device_id_type=MESH,
         )
@@ -522,16 +529,10 @@
         def _():
             part(spot, device).start()
 
-    @pl.loop(1, total)
-    def get_parts(step):
-        other = (spot + step) % total
-        part(other, other).wait_recv()
-
+    others = parts.at[pl.ds(0, total - 1), pl.ds(0, 1)]
+    pltpu.make_async_copy(others, others, part_sem.at[0]).wait()
+    pltpu.make_async_copy(others, others, part_sem.at[1]).wait()
     norm[...] = jnp.sum(parts[:, 0, :], axis=0, keepdims=True)
-
-    @pl.loop(1, total)
-    def sent_parts(step):
-        part(spot, (spot + step) % total).wait_send()
 
 
 def finish(product_in, norm_in, product_out, norm_out, value, sem):
@@ -590,8 +591,7 @@
                 pltpu.SemaphoreType.DMA((3, count)),
                 pltpu.SemaphoreType.DMA((count, width // block)),
                 pltpu.SemaphoreType.DMA((7 + width // block,)),
-                pltpu.SemaphoreType.DMA((count * cols,)),
-                pltpu.SemaphoreType.DMA((count * cols,)),
+                pltpu.SemaphoreType.DMA((2,)),
                 pltpu.SemaphoreType.DMA((2, cols, NEAR)),
                 pltpu.SemaphoreType.DMA((cols, NEAR)),
                 pltpu.SemaphoreType.DMA((2,)),

time: 33.9 us -> 33 us (0.973)
  Pallas kernels: 33.1 us -> 32.2 us
    pallas_call x1, Pallas kernels: 32.3 us -> 31.4 us  [per_device(): pl.pallas_call(functools.partial(kernel, length, cols), out_shape=(pltpu....]
where the time goes in v6:
time: 33 us; the launch traced here: 32.8 us
  Pallas kernels  32.2 us (98%)
  between operations  0.64 us (2%)
    pallas_call x1, Pallas kernels, per_device(): pl.pallas_call(functools.partial(kernel, length, cols), out_shape=(pltpu....  31.4 us
    pallas_call x1, Pallas kernels, per_device(): pl.pallas_call(finish, out_shape=(jax.ShapeDtypeStruct((rows, width), jnp...  0.82 us

profile of v6, /device:TPU:0, one launch (start us, length us, event | category | flops | bytes accessed | tf_op | source)
XLA Modules:
  0.0 32.8 jit_solution(6484036346417336271)
XLA Ops:
  0.6 31.4 %shard_map.95 = (f32[256,512]{1,0:T(8,128)S(1)}, f32[1,128]{1,0:T(1,128)S(1)}) custom-call(f32[256,1024]{1,0:T(8,128)} %density.1, f32[128,512]{1,0:T(8,128)} %hamil_in.1, s32[2,8]{1,0:T(2,128)} %occ_p_in.1, s32[1,4]{1,0:T(1,128)} %occ_hp_in.1, s32[8]{0:T(128)} %window_in.1, s32[16]{0:T(128)} %row_window_in.1, s32[4]{0:T(128)} %slab_in.1, s32[782]{0:T(1024)} %groups_in.1), custom_call_target="tpu_custom_call" | custom-call | tf_op jit(solution)/shard_map/pallas_call | solution.py:568
  32.0 0.8 %shard_map.96 = (f32[256,512]{1,0:T(8,128)}, f32[1]{0:T(128)}) custom-call(f32[256,512]{1,0:T(8,128)S(1)} %get-tuple-element.6.product_in, f32[1,128]{1,0:T(1,128)S(1)} %get-tuple-element.7.norm_in), custom_call_target="tpu_custom_call" | custom-call | tf_op jit(solution)/shard_map/pallas_call | solution.py:617

commit v7 on v6

--- a/solution.py
+++ b/solution.py
@@ -421,12 +421,6 @@
                     here = slice(begin * block, (begin + GROUP) * block)
                     product[:, here] = product[:, here] + value
 
-                if far:
-
-                    @pl.when(is_last & (distance == last))
-                    def _():
-                        far_result().wait_recv()
-
     def forward_far(plane):
         far_to(mate, plane).wait_recv()
 
@@ -464,13 +458,12 @@
     product[...] = jnp.zeros_like(product)
     inner = jnp.int32((z > 0) & (z < last))
 
-    @pl.loop(0, length + 2)
+    @pl.loop(0, length + 1)
     def steps(distance):
-        @pl.loop(0, panels)
-        def lines(panel):
+        for panel in range(panels):
             pass_below(distance + 1, panel)
-            ahead = distance * panels + panel + panels // 2
-            pass_above(ahead // panels, ahead % panels)
+            ahead = panel + panels // 2
+            pass_above(distance + ahead // panels, ahead % panels)
 
         if far:
 
@@ -498,18 +491,21 @@
 
         add_terms(distance - 1 - inner)
 
+    def squares_of(panel):
+        part_of = product[:, panel * block : (panel + 1) * block]
+        return jnp.sum((part_of * part_of).reshape(part_of.shape[0] // 8, 8, block), axis=0)
+
+    mine = squares_of(1)
+    for panel in range(2, panels):
+        mine = mine + squares_of(panel)
     if far:
 
         @pl.when(is_last)
         def _():
+            far_result().wait_recv()
             product[:, 0:block] = product[:, 0:block] + far_part[...]
 
-    lane = 128
-    squares = product[...] * product[...]
-    squares = jnp.sum(squares.reshape(squares.shape[0] // 8, 8, width), axis=0)
-    mine = squares[:, :lane]
-    for panel in range(1, width // lane):
-        mine = mine + squares[:, panel * lane : (panel + 1) * lane]
+    mine = mine + squares_of(0)
     spot = me * cols + my_col
     parts[spot, 0:1] = jnp.sum(mine, axis=0, keepdims=True)
 

time: 33 us -> 32.6 us (0.988)
  Pallas kernels: 32.2 us -> 31.8 us
    pallas_call x1, Pallas kernels: 31.4 us -> 31 us  [per_device(): pl.pallas_call(functools.partial(kernel, length, cols), out_shape=(pltpu....]
where the time goes in v7:
time: 32.6 us; the launch traced here: 32.5 us
  Pallas kernels  31.8 us (98%)
  between operations  0.64 us (2%)
    pallas_call x1, Pallas kernels, per_device(): pl.pallas_call(functools.partial(kernel, length, cols), out_shape=(pltpu....  31 us
    pallas_call x1, Pallas kernels, per_device(): pl.pallas_call(finish, out_shape=(jax.ShapeDtypeStruct((rows, width), jnp...  0.82 us

profile of v7, /device:TPU:0, one launch (start us, length us, event | category | flops | bytes accessed | tf_op | source)
XLA Modules:
  0.0 32.5 jit_solution(3255177066957385372)
XLA Ops:
  0.6 31.0 %shard_map.95 = (f32[256,512]{1,0:T(8,128)S(1)}, f32[1,128]{1,0:T(1,128)S(1)}) custom-call(f32[256,1024]{1,0:T(8,128)} %density.1, f32[128,512]{1,0:T(8,128)} %hamil_in.1, s32[2,8]{1,0:T(2,128)} %occ_p_in.1, s32[1,4]{1,0:T(1,128)} %occ_hp_in.1, s32[8]{0:T(128)} %window_in.1, s32[16]{0:T(128)} %row_window_in.1, s32[4]{0:T(128)} %slab_in.1, s32[782]{0:T(1024)} %groups_in.1), custom_call_target="tpu_custom_call" | custom-call | tf_op jit(solution)/shard_map/pallas_call | solution.py:564
  31.6 0.8 %shard_map.96 = (f32[256,512]{1,0:T(8,128)}, f32[1]{0:T(128)}) custom-call(f32[256,512]{1,0:T(8,128)S(1)} %get-tuple-element.6.product_in, f32[1,128]{1,0:T(1,128)S(1)} %get-tuple-element.7.norm_in), custom_call_target="tpu_custom_call" | custom-call | tf_op jit(solution)/shard_map/pallas_call | solution.py:613

commit v8 on v7

--- a/solution.py
+++ b/solution.py
@@ -14,7 +14,7 @@
 NEAR = 2
 CORES = 2
 GROUP = 2
-FAR_AFTER = 1
+FAR_AFTER = 0
 
 
 def kernel(
@@ -456,21 +456,22 @@
         far_result().start()
 
     product[...] = jnp.zeros_like(product)
-    inner = jnp.int32((z > 0) & (z < last))
+    inner = 0
 
     @pl.loop(0, length + 1)
     def steps(distance):
         for panel in range(panels):
             pass_below(distance + 1, panel)
+            if far and panel >= panels - NEAR:
+
+                @pl.when(is_near & (distance == 0))
+                def _():
+                    forward_far(panel - panels + NEAR)
+
             ahead = panel + panels // 2
             pass_above(distance + ahead // panels, ahead % panels)
 
         if far:
-
-            @pl.when(is_near & (distance == 0))
-            def _():
-                for plane in range(NEAR):
-                    forward_far(plane)
 
             @pl.when(is_near & (distance == 1))
             def _():

time: 32.6 us -> 32.4 us (level)
  no operation moved by 1% of the time
where the time goes in v8:
time: 32.4 us; the launch traced here: 32.3 us
  Pallas kernels  31.6 us (98%)
  between operations  0.64 us (2%)
    pallas_call x1, Pallas kernels, per_device(): pl.pallas_call(functools.partial(kernel, length, cols), out_shape=(pltpu....  30.8 us
    pallas_call x1, Pallas kernels, per_device(): pl.pallas_call(finish, out_shape=(jax.ShapeDtypeStruct((rows, width), jnp...  0.82 us

profile of v8, /device:TPU:0, one launch (start us, length us, event | category | flops | bytes accessed | tf_op | source)
XLA Modules:
  0.0 32.3 jit_solution(12029586658612173494)
XLA Ops:
  0.6 30.8 %shard_map.95 = (f32[256,512]{1,0:T(8,128)S(1)}, f32[1,128]{1,0:T(1,128)S(1)}) custom-call(f32[256,1024]{1,0:T(8,128)} %density.1, f32[128,512]{1,0:T(8,128)} %hamil_in.1, s32[2,8]{1,0:T(2,128)} %occ_p_in.1, s32[1,4]{1,0:T(1,128)} %occ_hp_in.1, s32[8]{0:T(128)} %window_in.1, s32[16]{0:T(128)} %row_window_in.1, s32[4]{0:T(128)} %slab_in.1, s32[782]{0:T(1024)} %groups_in.1), custom_call_target="tpu_custom_call" | custom-call | tf_op jit(solution)/shard_map/pallas_call | solution.py:565
  31.5 0.8 %shard_map.96 = (f32[256,512]{1,0:T(8,128)}, f32[1]{0:T(128)}) custom-call(f32[256,512]{1,0:T(8,128)S(1)} %get-tuple-element.6.product_in, f32[1,128]{1,0:T(1,128)S(1)} %get-tuple-element.7.norm_in), custom_call_target="tpu_custom_call" | custom-call | tf_op jit(solution)/shard_map/pallas_call | solution.py:614

commit v9 on v8

--- a/solution.py
+++ b/solution.py
@@ -468,15 +468,12 @@
                 def _():
                     forward_far(panel - panels + NEAR)
 
+                @pl.when(is_near & (distance == 1))
+                def _():
+                    mate_far(panel - panels + NEAR)
+
             ahead = panel + panels // 2
             pass_above(distance + ahead // panels, ahead % panels)
-
-        if far:
-
-            @pl.when(is_near & (distance == 1))
-            def _():
-                for plane in range(NEAR):
-                    mate_far(plane)
 
         pass_low_end(distance)
         pass_high_end(distance)
@@ -503,7 +500,7 @@
 
         @pl.when(is_last)
         def _():
-            far_result().wait_recv()
+            pltpu.make_async_copy(far_part, far_part, far_sem.at[1]).wait()
             product[:, 0:block] = product[:, 0:block] + far_part[...]
 
     mine = mine + squares_of(0)

time: 32.4 us -> 32.4 us (level)
  no operation moved by 1% of the time
where the time goes in v9:
time: 32.4 us; the launch traced here: 32.2 us
  Pallas kernels  31.6 us (98%)
  between operations  0.64 us (2%)
    pallas_call x1, Pallas kernels, per_device(): pl.pallas_call(functools.partial(kernel, length, cols), out_shape=(pltpu....  30.7 us
    pallas_call x1, Pallas kernels, per_device(): pl.pallas_call(finish, out_shape=(jax.ShapeDtypeStruct((rows, width), jnp...  0.82 us

profile of v9, /device:TPU:0, one launch (start us, length us, event | category | flops | bytes accessed | tf_op | source)
XLA Modules:
  0.0 32.2 jit_solution(11094205631855723414)
XLA Ops:
  0.6 30.7 %shard_map.95 = (f32[256,512]{1,0:T(8,128)S(1)}, f32[1,128]{1,0:T(1,128)S(1)}) custom-call(f32[256,1024]{1,0:T(8,128)} %density.1, f32[128,512]{1,0:T(8,128)} %hamil_in.1, s32[2,8]{1,0:T(2,128)} %occ_p_in.1, s32[1,4]{1,0:T(1,128)} %occ_hp_in.1, s32[8]{0:T(128)} %window_in.1, s32[16]{0:T(128)} %row_window_in.1, s32[4]{0:T(128)} %slab_in.1, s32[782]{0:T(1024)} %groups_in.1), custom_call_target="tpu_custom_call" | custom-call | tf_op jit(solution)/shard_map/pallas_call | solution.py:562
  31.4 0.8 %shard_map.96 = (f32[256,512]{1,0:T(8,128)}, f32[1]{0:T(128)}) custom-call(f32[256,512]{1,0:T(8,128)S(1)} %get-tuple-element.6.product_in, f32[1,128]{1,0:T(1,128)S(1)} %get-tuple-element.7.norm_in), custom_call_target="tpu_custom_call" | custom-call | tf_op jit(solution)/shard_map/pallas_call | solution.py:611
